TPU v7x, 32 devices: a whole 2x2x4 slice. The times are simulated.
32 devices in a mesh: wide: 8 (over z, core), narrow: 4 (over y, x).
Axes of the slice: x: 2, y: 2, z: 4, core: 2. Of those that a mesh axis runs over, the one named last changes fastest.
Arguments:
- features: bfloat16 [8192, 128], P(('wide', 'narrow')), may hold values from -6 to 6
- block_values: bfloat16 [4, 8, 96, 128, 128], P('narrow', 'wide'), may hold values from -0.125 to 0.125
- block_rows: int32 [4, 8, 96], P('narrow', 'wide'), may hold values from 0 to 15
- block_cols: int32 [4, 8, 96], P('narrow', 'wide'), may hold values from 0 to 7
- counts: int32 [4, 8], P('narrow', 'wide'), may hold values from 1 to 96, as said below
- weight: bfloat16 [128, 256], replicated, may hold values from -0.5 to 0.5
- bias: float32 [256], replicated, may hold values from -3 to 3
Outputs:
- activations: bfloat16 [8192, 256], P(('narrow', 'wide'))
Inputs may be any that keep to these rules, and one draw needn't show every extreme that they name: `counts`: each draw has a tile with all 96 slots used.
All inputs are finite; a program needn't handle non-finite values.
Results may differ from a plain program's by a relative error of at most 0.0046.
Values may be sent and summed in bfloat16 or wider, within the bound.
A program may use at most 64 MiB of HBM per device.

v0:
```python
import jax
import jax.numpy as jnp
from jax import lax
from jax.sharding import PartitionSpec as P


def shards(features, block_values, block_rows, block_cols, counts, weight, bias):
    local_nodes = features.shape[0]
    feature_width = features.shape[1]
    block_size = block_values.shape[-1]
    slot_count = block_values.shape[2]
    wide_count = lax.axis_size("wide")
    narrow_count = lax.axis_size("narrow")
    tile_blocks = wide_count * local_nodes // block_size
    panel_blocks = narrow_count * local_nodes // block_size
    values = block_values[0, 0]
    rows = block_rows[0, 0]
    cols = block_cols[0, 0]
    used = counts[0, 0]
    column_panel = lax.all_gather(features, "narrow", axis=0, tiled=True)
    panel_shaped = column_panel.reshape(panel_blocks, block_size, feature_width)
    picked = panel_shaped[cols]
    products = jnp.einsum("kij,kjf->kif", values, picked, preferred_element_type=jnp.float32)
    active = (jnp.arange(slot_count, dtype=jnp.int32) < used).astype(jnp.float32)
    flattened = (products * active[:, None, None]).reshape(slot_count, block_size * feature_width)
    selector = (rows[None, :] == jnp.arange(tile_blocks, dtype=jnp.int32)[:, None]).astype(
        jnp.float32
    )
    partial_value = jnp.dot(selector, flattened, precision=lax.Precision.HIGHEST)
    partial_value = partial_value.reshape(tile_blocks * block_size, feature_width)
    aggregated = lax.psum_scatter(partial_value, "wide", scatter_dimension=0, tiled=True)
    hidden = aggregated.astype(jnp.bfloat16)
    mixed = jnp.dot(hidden, weight, preferred_element_type=jnp.float32) + bias
    return jnp.maximum(mixed, 0.0).astype(jnp.bfloat16)


def solution(mesh):
    placed = (
        P(("wide", "narrow"), None),
        P("narrow", "wide", None, None, None),
        P("narrow", "wide", None),
        P("narrow", "wide", None),
        P("narrow", "wide"),
        P(),
        P(),
    )
    return jax.shard_map(
        shards, mesh=mesh, in_specs=placed, out_specs=P(("narrow", "wide"), None), check_vma=False
    )
```

profile of v0, /device:TPU:0, one launch (start us, length us, event | category | flops | bytes accessed | tf_op | source)
XLA Modules:
  0.0 87.8 jit_solution(6176407327379621510)
XLA Ops:
  6.5 0.0 copy-start
  6.5 0.0 reduce-scatter.2.cloned.1.call-start
  7.4 0.8 fusion.11
  8.2 10.7 %all_gather.3 = bf16[1024,128]{1,0:T(8,128)(2,1)S(1)} all-gather(bf16[256,128]{1,0:T(8,128)(2,1)} %param.7), channel_id=1, replica_groups=mesh['wide'=8,'narrow'=4] {'narrow'}, dimensions={0}, use_global_device_ids=true | all-gather | bytes 327680 | tf_op jit(solution)/shard_map/all_gather | solution.py:20
  18.9 2.7 %gather_fusion = bf16[96,128,128]{2,1,0:T(8,128)(2,1)} fusion(bf16[8,128,128]{2,1,0:T(8,128)(2,1)S(1)} %bitcast.21, s32[1024]{0:T(1024)S(1)} %pad_clamp_fusion), kind=kCustom, calls=%fused_computation | custom fusion | bytes 6291840 | tf_op jit(solution)/shard_map/gather | solution.py:22
  21.6 0.0 copy-done
  21.6 6.9 %multiply_bitcast_fusion = f32[96,128,128]{1,2,0:T(8,128)} fusion(f32[96]{0:T(128)S(1)} %compare_convert_fusion, bf16[96,128,128]{2,1,0:T(8,128)(2,1)} %gather_fusion, bf16[1,1,96,128,128]{4,3,2,1,0:T(8,128)(2,1)S(1)} %copy-done), kind=kOutput, calls=%fused_computation.4 | convolution fusion | flops 404226048 | bytes 12583296 | tf_op jit(solution)/shard_map/kij,kjf->kif/dot_general | solution.py:23
  28.5 0.0 copy-start.3
  28.5 6.5 %copy.9 = f32[96,128,128]{2,1,0:T(8,128)} copy(f32[96,128,128]{1,2,0:T(8,128)} %multiply_bitcast_fusion) | data formatting | bytes 12582912 | tf_op jit(solution)/shard_map/mul | solution.py:25
  35.1 0.0 copy-done.3
  35.1 9.1 %fusion = f32[16,16384]{1,0:T(8,128)} fusion(f32[12,8,128,128]{3,2,1,0:T(8,128)} %bitcast.22, s32[96]{0:T(128)S(1)} %bitcast.23), kind=kOutput, calls=%fused_computation.1 | convolution fusion | flops 301991424 | bytes 7340416 | tf_op jit(solution)/shard_map/dot_general | solution.py:29
  44.1 0.0 copy-start.1
  44.1 0.0 copy-start.2
  44.2 2.4 %reshape.46 = f32[2048,128]{1,0:T(8,128)} reshape(f32[16,16384]{1,0:T(8,128)} %fusion) | data formatting | bytes 2097152 | tf_op jit(solution)/shard_map/reshape | solution.py:30
  46.6 0.0 reduce-scatter.2.cloned.1.call-update
  46.6 32.6 %reduce-scatter.2.cloned.1.call-done = f32[256,128]{1,0:T(8,128)} async-done(((f32[2048,128]{1,0:T(8,128)}), f32[256,128]{1,0:T(8,128)}) %reduce-scatter.2.cloned.1.call-update) | async-done | bytes 131088 | tf_op jit(solution)/shard_map/reduce_scatter | solution.py:31
  79.2 0.0 copy-done.1
  79.2 0.0 copy-done.2
  79.2 1.7 %fusion.8 = bf16[256,256]{1,0:T(8,128)(2,1)} fusion(bf16[128,256]{1,0:T(8,128)(2,1)S(1)} %copy-done.1, f32[256]{0:T(256)S(1)} %copy-done.2, f32[256,128]{1,0:T(8,128)} %reduce-scatter.2.cloned.1.call-done), kind=kOutput, calls=%fused_computation.9 | convolution fusion | flops 17006592 | bytes 328704 | tf_op jit(solution)/shard_map/dot_general | solution.py:33
  (2 shorter events, 0.0 us)
Async XLA Ops:
  6.5 15.1 %copy-start = (bf16[1,1,96,128,128]{4,3,2,1,0:T(8,128)(2,1)S(1)}, bf16[1,1,96,128,128]{4,3,2,1,0:T(8,128)(2,1)}, u32[]{:S(2)}) copy-start(bf16[1,1,96,128,128]{4,3,2,1,0:T(8,128)(2,1)} %param.8) | copy-start | bytes 9437188
  6.5 72.7 %reduce-scatter.2.cloned.1.call-start = ((), (), s32[]{:S(2)}) async-start(), calls=%async_computation.1 | async-start | bytes 1179648 | tf_op jit(solution)/shard_map/reduce_scatter | solution.py:31
  28.5 6.5 %copy-start.3 = (s32[1,1,96]{2,1,0:T(1,128)S(1)}, s32[1,1,96]{2,1,0:T(1,128)}, u32[]{:S(2)}) copy-start(s32[1,1,96]{2,1,0:T(1,128)} %param.9) | copy-start | bytes 1156
  44.1 35.1 %copy-start.1 = (bf16[128,256]{1,0:T(8,128)(2,1)S(1)}, bf16[128,256]{1,0:T(8,128)(2,1)}, u32[]{:S(2)}) copy-start(bf16[128,256]{1,0:T(8,128)(2,1)} %param.12) | copy-start | bytes 196612
  44.1 35.1 %copy-start.2 = (f32[256]{0:T(256)S(1)}, f32[256]{0:T(256)}, u32[]{:S(2)}) copy-start(f32[256]{0:T(256)} %param.13) | copy-start | bytes 3076
Sparse Core Ops, SparseCore 0:
  46.7 32.4 reduce-scatter.1
where the time goes:
time: 88.1 us; the launch traced here: 87.8 us
  waiting for transfers between devices  32.6 us (37%)
  matrix products  17.7 us (20%)
  between operations  14.2 us (16%)
  local copies, waits for them, and re-layouts  11.7 us (13%)
  blocking collectives  10.7 us (12%)
    reduce_scatter x1, waiting for transfers between devices, shards(): lax.psum_scatter(partial_value, 'wide', scatter_dimension=0, tiled=True)  32.6 us
    all_gather x1, blocking collectives, shards(): column_panel = lax.all_gather(features, 'narrow', axis=0, tiled=True)  10.7 us
    dot_general x1, matrix products, shards(): jnp.dot(selector, flattened, precision=lax.Precision.HIGHEST)  9.07 us
    dot_general x1, matrix products, shards(): jnp.einsum('kij,kjf->kif', values, picked, preferred_element_type=jnp.flo...  6.91 us
    mul x1, local copies, waits for them, and re-layouts, shards(): products * active[:, None, None]  6.54 us
    gather x1, local copies, waits for them, and re-layouts, shards(): picked = panel_shaped[cols]  2.75 us
    reshape x1, local copies, waits for them, and re-layouts, shards(): partial_value.reshape(tile_blocks * block_size, feature_width)  2.42 us
  transfers between devices with their start and end apart: 1, of which 1 were waited for; matrix products, arithmetic and copies ran while one was open for 0% of the time, Pallas kernels for 0%

commit v1 on v0

v1 whole, which is shorter than its diff:
```python
import functools

import jax
import jax.numpy as jnp
from jax import lax
from jax.experimental import pallas as pl
from jax.experimental.pallas import tpu as pltpu
from jax.sharding import PartitionSpec as P

MESH = pl.DeviceIdType.MESH


def bits_for(count):
    return max(1, (count - 1).bit_length())


def group_steps(groups):
    if groups % 2 == 0:
        half = groups // 2
        pairs = [(1, low) for low in range(half)] + [(0, low) for low in range(1, half)] + [(0, 0)]
        return half, pairs
    return groups, [(0, low) for low in range(1, groups)] + [(0, 0)]


def kernel(
    wide_count, narrow_count,
    features, values, rows_in, cols_in, counts, weight, bias,
    out,
    panel, blocks, running, order_v, order_s, pair_out, pair_in, line_out, line_in,
    values_sem, own_sem, order_sem, feat_send, feat_recv, pair_send, pair_recv, line_send, line_recv,
):
    per_device, block, width = features.shape
    slots = blocks.shape[0] - 1
    entries = running.shape[1]
    phases = running.shape[0]
    part = block // phases
    tile_rows = wide_count * per_device
    panel_blocks = narrow_count * per_device
    groups = wide_count // 2
    half, steps = group_steps(groups)
    lanes = order_v.shape[1]
    col_shift = bits_for(lanes)
    row_shift = col_shift + bits_for(panel_blocks)

    wide = lax.axis_index("wide")
    narrow = lax.axis_index("narrow")
    group = lax.div(wide, 2)
    core = lax.rem(wide, 2)
    other = 1 - core
    high, low = lax.div(group, half), lax.rem(group, half)
    targets = [
        lax.rem(high + up, 2) * half + lax.rem(low + along, half) if groups % 2 == 0 else lax.rem(group + along, groups)
        for up, along in steps
    ]
    peers = [lax.rem(narrow + offset, narrow_count) for offset in range(1, narrow_count)]

    chunks = values_sem.shape[0]
    chunk = slots // chunks
    value_copies = [
        pltpu.make_async_copy(
            values.at[0, 0, pl.ds(i * chunk, chunk)], blocks.at[pl.ds(1 + i * chunk, chunk)], values_sem.at[i]
        )
        for i in range(chunks)
    ]
    own_copy = pltpu.make_async_copy(features, panel.at[pl.ds(narrow * per_device, per_device)], own_sem)
    for copy in value_copies:
        copy.start()
    own_copy.start()

    barrier = pltpu.get_barrier_semaphore()
    for peer in peers:
        pl.semaphore_signal(barrier, inc=1, device_id={"narrow": peer}, device_id_type=MESH)
    pl.semaphore_signal(barrier, inc=1, device_id={"wide": group * 2 + other}, device_id_type=MESH)
    for target in targets[:-1]:
        pl.semaphore_signal(barrier, inc=1, device_id={"wide": target * 2 + core}, device_id_type=MESH)

    blocks[0] = jnp.zeros((block, block), blocks.dtype)
    lane = lax.broadcasted_iota(jnp.int32, (1, lanes), 1)
    across = lax.broadcasted_iota(jnp.int32, (lanes, lanes), 1)
    down = lax.broadcasted_iota(jnp.int32, (lanes, lanes), 0)
    order_v[...] = jnp.broadcast_to((tile_rows << row_shift) + lane + 1, order_v.shape)
    slot = lane[:, :slots]
    row = jnp.where(slot < counts[...], rows_in[0], tile_rows)
    order_v[0:1, 0:slots] = (row << row_shift) + (cols_in[0] << col_shift) + slot + 1
    key = order_v[0:1, :]
    key_down = jnp.sum(jnp.where(down == across, key, 0), axis=1, keepdims=True)
    row_down = key_down >> row_shift
    held = jnp.sum((row_down == across).astype(jnp.int32), axis=0, keepdims=True)
    before = (key < key_down).astype(jnp.int32) + jnp.where(across < row_down, held & 1, 0)
    place = jnp.sum(before, axis=1, keepdims=True)
    ordered = jnp.sum(jnp.where((place == across) & (row_down < tile_rows), key_down, 0), axis=0, keepdims=True)
    first = (place & 1) == 0
    upto = jnp.sum(jnp.where((row_down <= across) & first, 1, 0), axis=0, keepdims=True)
    order_v[0:1, :] = ordered & ((1 << col_shift) - 1)
    order_v[1:2, :] = (ordered >> col_shift) & ((1 << (row_shift - col_shift)) - 1)
    order_v[2:3, :] = ordered >> row_shift
    order_v[3:4, :] = jnp.maximum(upto - 1, 0)
    order_v[4:5, :] = held
    order_copy = pltpu.make_async_copy(order_v, order_s, order_sem)
    order_copy.start()

    pl.semaphore_wait(barrier, (narrow_count - 1) + 1 + (groups - 1))

    feature_copies = []
    for i, peer in enumerate(peers):
        copy = pltpu.make_async_remote_copy(
            src_ref=features,
            dst_ref=panel.at[pl.ds(narrow * per_device, per_device)],
            send_sem=feat_send.at[i],
            recv_sem=feat_recv.at[i],
            device_id={"narrow": peer},
            device_id_type=MESH,
        )
        copy.start()
        feature_copies.append(copy)

    for copy in value_copies:
        copy.wait()
    own_copy.wait()
    order_copy.wait()
    for copy in feature_copies:
        copy.wait_recv()

    def sweep(phase, begin, end, total):
        here = pl.ds(phase * part, part)
        unroll = max(u for u in range(1, 9) if (end - begin) % u == 0)

        def some(step, total):
            for j in range(unroll):
                e = begin + step * unroll + j
                keep = jnp.where(order_s[2, 2 * e] == order_s[2, jnp.maximum(2 * e - 2, 0)], 1.0, 0.0)
                left = jnp.concatenate([blocks[order_s[0, 2 * e], here], blocks[order_s[0, 2 * e + 1], here]], axis=1)
                right = jnp.concatenate([panel[order_s[1, 2 * e]], panel[order_s[1, 2 * e + 1]]], axis=0)
                product = jnp.dot(left, right, preferred_element_type=jnp.float32)
                total = total * keep.astype(jnp.float32) + product
                running[phase, e] = total
            return total

        return lax.fori_loop(0, (end - begin) // unroll, some, total)

    def row_sum(phase, r):
        present = jnp.where(order_s[4, r] > 0, 1.0, 0.0).astype(jnp.float32)
        return running[phase, order_s[3, r]] * present

    pair_copies, line_copies, totals = [], [], []

    def send_pair(phase):
        for i, target in enumerate(targets):
            for j in range(per_device):
                pair_out[phase, i, j * part:(j + 1) * part, :] = row_sum(phase, (target * 2 + other) * per_device + j)
            copy = pltpu.make_async_remote_copy(
                src_ref=pair_out.at[phase, i],
                dst_ref=pair_in.at[phase, i],
                send_sem=pair_send.at[phase, i],
                recv_sem=pair_recv.at[phase, i],
                device_id={"wide": group * 2 + other},
                device_id_type=MESH,
            )
            copy.start()
            pair_copies.append(copy)

    def send_line(phase):
        for i, target in enumerate(targets):
            own = jnp.concatenate(
                [row_sum(phase, (target * 2 + core) * per_device + j) for j in range(per_device)], axis=0
            )
            pair_copies[phase * groups + i].wait_recv()
            both = own + pair_in[phase, i]
            if i == groups - 1:
                totals.append(both)
            else:
                line_out[phase, i] = both.astype(jnp.bfloat16)
                copy = pltpu.make_async_remote_copy(
                    src_ref=line_out.at[phase, i],
                    dst_ref=line_in.at[phase, i],
                    send_sem=line_send.at[phase, i],
                    recv_sem=line_recv.at[phase, i],
                    device_id={"wide": target * 2 + core},
                    device_id_type=MESH,
                )
                copy.start()
                line_copies.append(copy)

    middle = entries // 2
    for phase in range(phases):
        total = jnp.zeros((part, width), jnp.float32)
        if phase == 0:
            sweep(phase, 0, entries, total)
        else:
            total = sweep(phase, 0, middle, total)
            send_line(phase - 1)
            sweep(phase, middle, entries, total)
        send_pair(phase)
    send_line(phases - 1)

    for phase in range(phases):
        total = totals[phase]
        for i in range(groups - 1):
            line_copies[phase * (groups - 1) + i].wait_recv()
            total = total + line_in[phase, i].astype(jnp.float32)
        mixed = jnp.dot(total.astype(jnp.bfloat16), weight[...], preferred_element_type=jnp.float32) + bias[...]
        result = jnp.maximum(mixed, 0.0).astype(out.dtype)
        for j in range(per_device):
            out[pl.ds(j * block + phase * part, part), :] = result[j * part:(j + 1) * part]

    for copy in feature_copies + pair_copies + line_copies:
        copy.wait_send()


def shards(features, block_values, block_rows, block_cols, counts, weight, bias):
    wide_count = lax.axis_size("wide")
    narrow_count = lax.axis_size("narrow")
    nodes, width = features.shape
    slots, block = block_values.shape[2], block_values.shape[3]
    per_device = nodes // block
    groups = wide_count // 2
    hidden = weight.shape[1]
    tile_rows = wide_count * per_device
    entries = (slots + min(slots, tile_rows)) // 2
    lanes = -(-(slots + tile_rows) // 128) * 128
    phases = 2
    part_nodes = nodes // phases
    others_in_line = max(groups - 1, 1)
    chunks = max(c for c in (1, 2, 4) if slots % c == 0)
    others = max(narrow_count - 1, 1)
    in_vmem = pl.BlockSpec(memory_space=pltpu.VMEM)
    in_hbm = pl.BlockSpec(memory_space=pltpu.HBM)
    dma = pltpu.SemaphoreType.DMA
    return pl.pallas_call(
        functools.partial(kernel, wide_count, narrow_count),
        out_shape=jax.ShapeDtypeStruct((nodes, hidden), jnp.bfloat16),
        in_specs=[in_hbm, in_hbm] + [in_vmem] * 5,
        out_specs=in_vmem,
        scratch_shapes=[
            pltpu.VMEM((narrow_count * per_device, block, width), jnp.bfloat16),
            pltpu.VMEM((slots + 1, block, block), jnp.bfloat16),
            pltpu.VMEM((phases, entries, block // phases, width), jnp.float32),
            pltpu.VMEM((8, lanes), jnp.int32),
            pltpu.SMEM((8, lanes), jnp.int32),
            pltpu.VMEM((phases, groups, part_nodes, width), jnp.float32),
            pltpu.VMEM((phases, groups, part_nodes, width), jnp.float32),
            pltpu.VMEM((phases, others_in_line, part_nodes, width), jnp.bfloat16),
            pltpu.VMEM((phases, others_in_line, part_nodes, width), jnp.bfloat16),
            dma((chunks,)),
            dma,
            dma,
            dma((others,)),
            dma((others,)),
            dma((phases, groups)),
            dma((phases, groups)),
            dma((phases, others_in_line)),
            dma((phases, others_in_line)),
        ],
        compiler_params=pltpu.CompilerParams(
            collective_id=0, has_side_effects=True, vmem_limit_bytes=56 * 1024 * 1024
        ),
        cost_estimate=pl.CostEstimate(
            flops=2 * slots * block * block * width, bytes_accessed=2 * slots * block * block, transcendentals=0
        ),
    )(
        features.reshape(per_device, block, width), block_values, block_rows, block_cols, counts,
        weight, bias.reshape(1, hidden),
    )


def solution(mesh):
    placed = (
        P(("wide", "narrow"), None),
        P("narrow", "wide", None, None, None),
        P("narrow", "wide", None),
        P("narrow", "wide", None),
        P("narrow", "wide"),
        P(),
        P(),
    )
    return jax.shard_map(
        shards, mesh=mesh, in_specs=placed, out_specs=P(("narrow", "wide"), None), check_vma=False
    )
```

time: 88.1 us -> 24.2 us (0.27)
  waiting for transfers between devices: 32.6 us -> 0 us
  Pallas kernels: 0 us -> 21.8 us
  matrix products: 17.7 us -> 0 us
  between operations: 14.2 us -> 0.66 us
  blocking collectives: 10.7 us -> 0 us
  local copies, waits for them, and re-layouts: 11.7 us -> 1.57 us
    reduce_scatter x1 -> x0, waiting for transfers between devices: 32.6 us -> none  [shards(): lax.psum_scatter(partial_value, 'wide', scatter_dimension=0, tiled=True)]
    pallas_call x0 -> x1, Pallas kernels: none -> 21.8 us  [shards(): pl.pallas_call(functools.partial(kernel, wide_count, narrow_count), out_s...]
    dot_general x3 -> x0, matrix products: 17.7 us -> none  [the longest x1 9.07 us: shards(): jnp.dot(selector, flattened, precision=lax.Precision.HIGHEST)]
    all_gather x1 -> x0, blocking collectives: 10.7 us -> none  [shards(): column_panel = lax.all_gather(features, 'narrow', axis=0, tiled=True)]
    mul x1 -> x0, local copies, waits for them, and re-layouts: 6.54 us -> none  [shards(): products * active[:, None, None]]
    gather x1 -> x0, local copies, waits for them, and re-layouts: 2.75 us -> none  [shards(): picked = panel_shaped[cols]]
    reshape x1 -> x0, local copies, waits for them, and re-layouts: 2.42 us -> none  [shards(): partial_value.reshape(tile_blocks * block_size, feature_width)]
    unnamed x8 -> x1, local copies, waits for them, and re-layouts: 0.02 us -> 1.57 us
  transfers between devices with their start and end apart: 1 -> 0, of which waited for: 1 -> 0; matrix products, arithmetic and copies ran while one was open for 0% -> 0% of each run, Pallas kernels for 0% -> 0%
where the time goes in v1:
time: 24.2 us; the launch traced here: 24 us
  Pallas kernels  21.8 us (90%)
  local copies, waits for them, and re-layouts  1.57 us (6%)
  between operations  0.66 us (3%)
    pallas_call x1, Pallas kernels, shards(): pl.pallas_call(functools.partial(kernel, wide_count, narrow_count), out_s...  21.8 us
    unnamed x1, local copies, waits for them, and re-layouts  1.57 us

profile of v1, /device:TPU:0, one launch (start us, length us, event | category | flops | bytes accessed | tf_op | source)
XLA Modules:
  0.0 24.0 jit_solution(13703896114629068245)
XLA Ops:
  0.7 21.8 %shard_map.73 = bf16[256,256]{1,0:T(8,128)(2,1)} custom-call(bf16[2,128,128]{2,1,0:T(8,128)(2,1)} %bitcast.2, bf16[1,1,96,128,128]{4,3,2,1,0:T(8,128)(2,1)} %values.1, s32[1,1,96]{2,1,0:T(1,128)} %rows_in.1, s32[1,1,96]{2,1,0:T(1,128)} %cols_in.1, s32[1,1]{1,0:T(1,128)S(6)} %copy.9.counts, bf16[128,256]{1,0:T(8,128)(2,1)} %weight.1, f32[1,256]{1,0:T(1,128)} %bitcast.3), custom_call_target="tpu_custom_call" | custom-call | flops 402653184 | bytes 3145728 | tf_op jit(solution)/shard_map/pallas_call | solution.py:229
  22.5 1.6 %copy.10 = bf16[256,256]{1,0:T(8,128)(2,1)} copy(bf16[256,256]{1,0:T(8,128)(2,1)} %shard_map.73) | data formatting | bytes 262144

commit v2 on v1

--- a/solution.py
+++ b/solution.py
@@ -126,14 +126,17 @@
         unroll = max(u for u in range(1, 9) if (end - begin) % u == 0)
 
         def some(step, total):
+            products, keeps = [], []
             for j in range(unroll):
                 e = begin + step * unroll + j
                 keep = jnp.where(order_s[2, 2 * e] == order_s[2, jnp.maximum(2 * e - 2, 0)], 1.0, 0.0)
+                keeps.append(keep.astype(jnp.float32))
                 left = jnp.concatenate([blocks[order_s[0, 2 * e], here], blocks[order_s[0, 2 * e + 1], here]], axis=1)
                 right = jnp.concatenate([panel[order_s[1, 2 * e]], panel[order_s[1, 2 * e + 1]]], axis=0)
-                product = jnp.dot(left, right, preferred_element_type=jnp.float32)
-                total = total * keep.astype(jnp.float32) + product
-                running[phase, e] = total
+                products.append(jnp.dot(left, right, preferred_element_type=jnp.float32))
+            for j in range(unroll):
+                total = total * keeps[j] + products[j]
+                running[phase, begin + step * unroll + j] = total
             return total
 
         return lax.fori_loop(0, (end - begin) // unroll, some, total)

time: 24.2 us -> 24.2 us (level)
  no operation moved by 1% of the time
where the time goes in v2:
time: 24.2 us; the launch traced here: 24 us
  Pallas kernels  21.8 us (90%)
  local copies, waits for them, and re-layouts  1.57 us (6%)
  between operations  0.66 us (3%)
    pallas_call x1, Pallas kernels, shards(): pl.pallas_call(functools.partial(kernel, wide_count, narrow_count), out_s...  21.8 us
    unnamed x1, local copies, waits for them, and re-layouts  1.57 us

profile of v2, /device:TPU:0, one launch (start us, length us, event | category | flops | bytes accessed | tf_op | source)
XLA Modules:
  0.0 24.0 jit_solution(13703896114629068245)
XLA Ops:
  0.7 21.8 %shard_map.73 = bf16[256,256]{1,0:T(8,128)(2,1)} custom-call(bf16[2,128,128]{2,1,0:T(8,128)(2,1)} %bitcast.2, bf16[1,1,96,128,128]{4,3,2,1,0:T(8,128)(2,1)} %values.1, s32[1,1,96]{2,1,0:T(1,128)} %rows_in.1, s32[1,1,96]{2,1,0:T(1,128)} %cols_in.1, s32[1,1]{1,0:T(1,128)S(6)} %copy.9.counts, bf16[128,256]{1,0:T(8,128)(2,1)} %weight.1, f32[1,256]{1,0:T(1,128)} %bitcast.3), custom_call_target="tpu_custom_call" | custom-call | flops 402653184 | bytes 3145728 | tf_op jit(solution)/shard_map/pallas_call | solution.py:232
  22.5 1.6 %copy.10 = bf16[256,256]{1,0:T(8,128)(2,1)} copy(bf16[256,256]{1,0:T(8,128)(2,1)} %shard_map.73) | data formatting | bytes 262144

commit v3 on v1

v3 whole, which is shorter than its diff:
```python
import functools

import jax
import jax.numpy as jnp
from jax import lax
from jax.experimental import pallas as pl
from jax.experimental.pallas import tpu as pltpu
from jax.sharding import PartitionSpec as P

MESH = pl.DeviceIdType.MESH


def bits_for(count):
    return max(1, (count - 1).bit_length())


def group_steps(groups):
    if groups % 2 == 0:
        half = groups // 2
        pairs = [(1, low) for low in range(half)] + [(0, low) for low in range(1, half)] + [(0, 0)]
        return half, pairs
    return groups, [(0, low) for low in range(1, groups)] + [(0, 0)]


def slot_kernel(
    wide_count, narrow_count,
    features, values, rows_in, cols_in, counts, weight, bias,
    out,
    panel, blocks, running, order_v, order_s, pair_out, pair_in, line_out, line_in,
    values_sem, own_sem, order_sem, feat_send, feat_recv, pair_send, pair_recv, line_send, line_recv,
):
    per_device, block, width = features.shape
    slots = blocks.shape[0]
    tile_rows = wide_count * per_device
    panel_blocks = narrow_count * per_device
    groups = wide_count // 2
    half, steps = group_steps(groups)
    lanes = order_v.shape[1]
    col_shift = bits_for(lanes)
    row_shift = col_shift + bits_for(panel_blocks)

    wide = lax.axis_index("wide")
    narrow = lax.axis_index("narrow")
    group = lax.div(wide, 2)
    core = lax.rem(wide, 2)
    other = 1 - core
    high, low = lax.div(group, half), lax.rem(group, half)
    targets = [
        lax.rem(high + up, 2) * half + lax.rem(low + along, half) if groups % 2 == 0 else lax.rem(group + along, groups)
        for up, along in steps
    ]
    peers = [lax.rem(narrow + offset, narrow_count) for offset in range(1, narrow_count)]

    chunks = values_sem.shape[0]
    chunk = slots // chunks
    value_copies = [
        pltpu.make_async_copy(
            values.at[0, 0, pl.ds(i * chunk, chunk)], blocks.at[pl.ds(i * chunk, chunk)], values_sem.at[i]
        )
        for i in range(chunks)
    ]
    own_copy = pltpu.make_async_copy(features, panel.at[pl.ds(narrow * per_device, per_device)], own_sem)
    for copy in value_copies:
        copy.start()
    own_copy.start()

    barrier = pltpu.get_barrier_semaphore()
    for peer in peers:
        pl.semaphore_signal(barrier, inc=1, device_id={"narrow": peer}, device_id_type=MESH)
    pl.semaphore_signal(barrier, inc=1, device_id={"wide": group * 2 + other}, device_id_type=MESH)
    for target in targets[:-1]:
        pl.semaphore_signal(barrier, inc=1, device_id={"wide": target * 2 + core}, device_id_type=MESH)

    lane = lax.broadcasted_iota(jnp.int32, (1, lanes), 1)
    across = lax.broadcasted_iota(jnp.int32, (lanes, lanes), 1)
    down = lax.broadcasted_iota(jnp.int32, (lanes, lanes), 0)
    order_v[...] = jnp.broadcast_to((tile_rows << row_shift) + lane, order_v.shape)
    slot = lane[:, :slots]
    row = jnp.where(slot < counts[...], rows_in[0], tile_rows)
    order_v[0:1, 0:slots] = (row << row_shift) + (cols_in[0] << col_shift) + slot
    key = order_v[0:1, :]
    key_down = jnp.sum(jnp.where(down == across, key, 0), axis=1, keepdims=True)
    rank = jnp.sum((key < key_down).astype(jnp.int32), axis=1, keepdims=True)
    ordered = jnp.sum(jnp.where(rank == across, key_down, 0), axis=0, keepdims=True)
    row_down = key_down >> row_shift
    upto = jnp.sum((row_down <= across).astype(jnp.int32), axis=0, keepdims=True)
    held = jnp.sum((row_down == across).astype(jnp.int32), axis=0, keepdims=True)
    order_v[0:1, :] = ordered & ((1 << col_shift) - 1)
    order_v[1:2, :] = (ordered >> col_shift) & ((1 << (row_shift - col_shift)) - 1)
    order_v[2:3, :] = ordered >> row_shift
    order_v[3:4, :] = jnp.maximum(upto - 1, 0)
    order_v[4:5, :] = held
    order_copy = pltpu.make_async_copy(order_v, order_s, order_sem)
    order_copy.start()

    pl.semaphore_wait(barrier, (narrow_count - 1) + 1 + (groups - 1))

    feature_copies = []
    for i, peer in enumerate(peers):
        copy = pltpu.make_async_remote_copy(
            src_ref=features,
            dst_ref=panel.at[pl.ds(narrow * per_device, per_device)],
            send_sem=feat_send.at[i],
            recv_sem=feat_recv.at[i],
            device_id={"narrow": peer},
            device_id_type=MESH,
        )
        copy.start()
        feature_copies.append(copy)

    for copy in value_copies:
        copy.wait()
    own_copy.wait()
    order_copy.wait()
    for copy in feature_copies:
        copy.wait_recv()

    unroll = max(u for u in range(1, 9) if slots % u == 0)

    def sweep(step, total):
        for j in range(unroll):
            p = step * unroll + j
            before = jnp.maximum(p - 1, 0)
            keep = jnp.where(order_s[2, p] == order_s[2, before], 1.0, 0.0).astype(jnp.float32)
            product = jnp.dot(blocks[order_s[0, p]], panel[order_s[1, p]], preferred_element_type=jnp.float32)
            total = total * keep + product
            running[p] = total
        return total

    lax.fori_loop(0, slots // unroll, sweep, jnp.zeros((block, width), jnp.float32))

    def row_sum(r):
        present = jnp.where(order_s[4, r] > 0, 1.0, 0.0).astype(jnp.float32)
        return running[order_s[3, r]] * present

    pair_copies = []
    for i, target in enumerate(targets):
        for j in range(per_device):
            pair_out[i, j * block:(j + 1) * block, :] = row_sum((target * 2 + other) * per_device + j)
        copy = pltpu.make_async_remote_copy(
            src_ref=pair_out.at[i],
            dst_ref=pair_in.at[i],
            send_sem=pair_send.at[i],
            recv_sem=pair_recv.at[i],
            device_id={"wide": group * 2 + other},
            device_id_type=MESH,
        )
        copy.start()
        pair_copies.append(copy)

    line_copies = []
    total = None
    for i, target in enumerate(targets):
        own = jnp.concatenate(
            [row_sum((target * 2 + core) * per_device + j) for j in range(per_device)], axis=0
        )
        pair_copies[i].wait_recv()
        both = own + pair_in[i]
        if i == groups - 1:
            total = both
        else:
            line_out[i] = both.astype(jnp.bfloat16)
            copy = pltpu.make_async_remote_copy(
                src_ref=line_out.at[i],
                dst_ref=line_in.at[i],
                send_sem=line_send.at[i],
                recv_sem=line_recv.at[i],
                device_id={"wide": target * 2 + core},
                device_id_type=MESH,
            )
            copy.start()
            line_copies.append(copy)

    for i, copy in enumerate(line_copies):
        copy.wait_recv()
        total = total + line_in[i].astype(jnp.float32)
    mixed = jnp.dot(total.astype(jnp.bfloat16), weight[...], preferred_element_type=jnp.float32) + bias[...]
    out[...] = jnp.maximum(mixed, 0.0).astype(out.dtype)

    for copy in feature_copies + pair_copies + line_copies:
        copy.wait_send()


def dense_kernel(
    wide_count, narrow_count,
    features, values, rows_in, cols_in, counts, weight, bias,
    out,
    panel, blocks, running, dense, sums, order_v, order_s, pair_out, pair_in, line_out, line_in,
    values_sem, own_sem, order_sem, feat_send, feat_recv, pair_send, pair_recv, line_send, line_recv,
):
    nodes, width = features.shape
    slots, block = blocks.shape[0], blocks.shape[1]
    per_device = nodes // block
    tile_rows = wide_count * per_device
    panel_blocks = narrow_count * per_device
    spots = tile_rows * panel_blocks
    groups = wide_count // 2
    half, steps = group_steps(groups)
    lanes = order_v.shape[1]
    shift = bits_for(lanes)

    wide = lax.axis_index("wide")
    narrow = lax.axis_index("narrow")
    group = lax.div(wide, 2)
    core = lax.rem(wide, 2)
    other = 1 - core
    high, low = lax.div(group, half), lax.rem(group, half)
    targets = [
        lax.rem(high + up, 2) * half + lax.rem(low + along, half) if groups % 2 == 0 else lax.rem(group + along, groups)
        for up, along in steps
    ]
    peers = [lax.rem(narrow + offset, narrow_count) for offset in range(1, narrow_count)]

    chunks = values_sem.shape[0]
    chunk = slots // chunks
    value_copies = [
        pltpu.make_async_copy(
            values.at[0, 0, pl.ds(i * chunk, chunk)], blocks.at[pl.ds(i * chunk, chunk)], values_sem.at[i]
        )
        for i in range(chunks)
    ]
    own_copy = pltpu.make_async_copy(features, panel.at[narrow], own_sem)
    for copy in value_copies:
        copy.start()
    own_copy.start()

    barrier = pltpu.get_barrier_semaphore()
    for peer in peers:
        pl.semaphore_signal(barrier, inc=1, device_id={"narrow": peer}, device_id_type=MESH)
    pl.semaphore_signal(barrier, inc=1, device_id={"wide": group * 2 + other}, device_id_type=MESH)
    for target in targets[:-1]:
        pl.semaphore_signal(barrier, inc=1, device_id={"wide": target * 2 + core}, device_id_type=MESH)

    lane = lax.broadcasted_iota(jnp.int32, (1, lanes), 1)
    across = lax.broadcasted_iota(jnp.int32, (lanes, lanes), 1)
    down = lax.broadcasted_iota(jnp.int32, (lanes, lanes), 0)
    order_v[...] = jnp.broadcast_to((spots << shift) + lane, order_v.shape)
    slot = lane[:, :slots]
    spot = jnp.where(slot < counts[...], rows_in[0] * panel_blocks + cols_in[0], spots)
    order_v[0:1, 0:slots] = (spot << shift) + slot
    key = order_v[0:1, :]
    key_down = jnp.sum(jnp.where(down == across, key, 0), axis=1, keepdims=True)
    rank = jnp.sum((key < key_down).astype(jnp.int32), axis=1, keepdims=True)
    ordered = jnp.sum(jnp.where(rank == across, key_down, 0), axis=0, keepdims=True)
    spot_down = key_down >> shift
    upto = jnp.sum((spot_down <= across).astype(jnp.int32), axis=0, keepdims=True)
    held = jnp.sum((spot_down == across).astype(jnp.int32), axis=0, keepdims=True)
    order_v[0:1, :] = ordered & ((1 << shift) - 1)
    order_v[1:2, :] = ordered >> shift
    order_v[2:3, :] = jnp.where(held > 0, upto, 0)
    order_copy = pltpu.make_async_copy(order_v, order_s, order_sem)
    order_copy.start()

    pl.semaphore_wait(barrier, (narrow_count - 1) + 1 + (groups - 1))

    feature_copies = []
    for i, peer in enumerate(peers):
        copy = pltpu.make_async_remote_copy(
            src_ref=features,
            dst_ref=panel.at[narrow],
            send_sem=feat_send.at[i],
            recv_sem=feat_recv.at[i],
            device_id={"narrow": peer},
            device_id_type=MESH,
        )
        copy.start()
        feature_copies.append(copy)

    running[0] = jnp.zeros((block, block), running.dtype)
    order_copy.wait()
    for copy in value_copies:
        copy.wait()
    unroll = max(u for u in range(1, 9) if slots % u == 0)

    def sweep(step, total):
        for j in range(unroll):
            p = step * unroll + j
            keep = jnp.where(order_s[1, p] == order_s[1, jnp.maximum(p - 1, 0)], 1.0, 0.0)
            total = total * keep.astype(jnp.float32) + blocks[order_s[0, p]].astype(jnp.float32)
            running[p + 1] = total.astype(running.dtype)
        return total

    lax.fori_loop(0, slots // unroll, sweep, jnp.zeros((block, block), jnp.float32))

    def place(r, carry):
        for c in range(panel_blocks):
            dense[c // per_device, pl.ds(pl.multiple_of(r * block, block), block),
                  (c % per_device) * block:(c % per_device + 1) * block] = running[order_s[2, r * panel_blocks + c]]
        return carry

    lax.fori_loop(0, tile_rows, place, 0)

    own_copy.wait()
    sources = [narrow] + [lax.rem(narrow + narrow_count - offset, narrow_count) for offset in range(1, narrow_count)]
    turns = [0] + list(range(1, narrow_count - 1, 2)) + list(range(narrow_count - 1, 0, -2))
    turns = list(dict.fromkeys(turns + list(range(narrow_count))))
    for n, turn in enumerate(turns[:-1]):
        if turn:
            feature_copies[turn - 1].wait_recv()
        source = sources[turn]

        def multiply(d, carry):
            here = pl.ds(pl.multiple_of(d * nodes, nodes), nodes)
            product = jnp.dot(dense[source, here], panel[source], preferred_element_type=jnp.float32)
            sums[here] = product if n == 0 else sums[here] + product
            return carry

        lax.fori_loop(0, wide_count, multiply, 0, unroll=True)
    if turns[-1]:
        feature_copies[turns[-1] - 1].wait_recv()
    final = sources[turns[-1]]

    def chunk_sum(d):
        here = pl.ds(pl.multiple_of(d * nodes, nodes), nodes)
        product = jnp.dot(dense[final, here], panel[final], preferred_element_type=jnp.float32)
        return product + sums[here] if narrow_count > 1 else product

    pair_copies = []
    for i, target in enumerate(targets):
        pair_out[i] = chunk_sum(target * 2 + other)
        copy = pltpu.make_async_remote_copy(
            src_ref=pair_out.at[i],
            dst_ref=pair_in.at[i],
            send_sem=pair_send.at[i],
            recv_sem=pair_recv.at[i],
            device_id={"wide": group * 2 + other},
            device_id_type=MESH,
        )
        copy.start()
        pair_copies.append(copy)

    line_copies = []
    total = None
    for i, target in enumerate(targets):
        own = chunk_sum(target * 2 + core)
        pair_copies[i].wait_recv()
        both = own + pair_in[i]
        if i == groups - 1:
            total = both
        else:
            line_out[i] = both.astype(jnp.bfloat16)
            copy = pltpu.make_async_remote_copy(
                src_ref=line_out.at[i],
                dst_ref=line_in.at[i],
                send_sem=line_send.at[i],
                recv_sem=line_recv.at[i],
                device_id={"wide": target * 2 + core},
                device_id_type=MESH,
            )
            copy.start()
            line_copies.append(copy)

    for i, copy in enumerate(line_copies):
        copy.wait_recv()
        total = total + line_in[i].astype(jnp.float32)
    mixed = jnp.dot(total.astype(jnp.bfloat16), weight[...], preferred_element_type=jnp.float32) + bias[...]
    out[...] = jnp.maximum(mixed, 0.0).astype(out.dtype)

    for copy in feature_copies + pair_copies + line_copies:
        copy.wait_send()


DENSE_BYTES = 8 * 1024 * 1024


def shards(features, block_values, block_rows, block_cols, counts, weight, bias):
    wide_count = lax.axis_size("wide")
    narrow_count = lax.axis_size("narrow")
    nodes, width = features.shape
    slots, block = block_values.shape[2], block_values.shape[3]
    per_device = nodes // block
    groups = wide_count // 2
    hidden = weight.shape[1]
    tile_rows = wide_count * per_device
    panel_blocks = narrow_count * per_device
    dense_fits = tile_rows * panel_blocks * block * block * 2 <= DENSE_BYTES
    keys = tile_rows * panel_blocks if dense_fits else tile_rows
    lanes = -(-max(slots, keys) // 128) * 128
    chunks = max(c for c in (1, 2, 4) if slots % c == 0)
    others = max(narrow_count - 1, 1)
    in_vmem = pl.BlockSpec(memory_space=pltpu.VMEM)
    in_hbm = pl.BlockSpec(memory_space=pltpu.HBM)
    dma = pltpu.SemaphoreType.DMA
    return pl.pallas_call(
        functools.partial(dense_kernel if dense_fits else slot_kernel, wide_count, narrow_count),
        out_shape=jax.ShapeDtypeStruct((nodes, hidden), jnp.bfloat16),
        in_specs=[in_hbm, in_hbm] + [in_vmem] * 5,
        out_specs=in_vmem,
        scratch_shapes=[
            *(
                [
                    pltpu.VMEM((narrow_count, nodes, width), jnp.bfloat16),
                    pltpu.VMEM((slots, block, block), jnp.bfloat16),
                    pltpu.VMEM((slots + 1, block, block), jnp.bfloat16),
                    pltpu.VMEM((narrow_count, wide_count * nodes, nodes), jnp.bfloat16),
                    pltpu.VMEM((wide_count * nodes, width), jnp.float32),
                ]
                if dense_fits
                else [
                    pltpu.VMEM((panel_blocks, block, width), jnp.bfloat16),
                    pltpu.VMEM((slots, block, block), jnp.bfloat16),
                    pltpu.VMEM((slots, block, width), jnp.float32),
                ]
            ),
            pltpu.VMEM((8, lanes), jnp.int32),
            pltpu.SMEM((8, lanes), jnp.int32),
            pltpu.VMEM((groups, nodes, width), jnp.float32),
            pltpu.VMEM((groups, nodes, width), jnp.float32),
            pltpu.VMEM((max(groups - 1, 1), nodes, width), jnp.bfloat16),
            pltpu.VMEM((max(groups - 1, 1), nodes, width), jnp.bfloat16),
            dma((chunks,)),
            dma,
            dma,
            dma((others,)),
            dma((others,)),
            dma((groups,)),
            dma((groups,)),
            dma((max(groups - 1, 1),)),
            dma((max(groups - 1, 1),)),
        ],
        compiler_params=pltpu.CompilerParams(
            collective_id=0 if dense_fits else 1, has_side_effects=True, vmem_limit_bytes=56 * 1024 * 1024
        ),
        cost_estimate=pl.CostEstimate(
            flops=2 * slots * block * block * width, bytes_accessed=2 * slots * block * block, transcendentals=0
        ),
    )(
        features if dense_fits else features.reshape(per_device, block, width), block_values, block_rows, block_cols, counts,
        weight, bias.reshape(1, hidden),
    )


def solution(mesh):
    placed = (
        P(("wide", "narrow"), None),
        P("narrow", "wide", None, None, None),
        P("narrow", "wide", None),
        P("narrow", "wide", None),
        P("narrow", "wide"),
        P(),
        P(),
    )
    return jax.shard_map(
        shards, mesh=mesh, in_specs=placed, out_specs=P(("narrow", "wide"), None), check_vma=False
    )
```

time: 24.2 us -> 22.8 us (0.942)
  Pallas kernels: 21.8 us -> 20.4 us
    pallas_call x1, Pallas kernels: 21.8 us -> 20.4 us  [shards(): pl.pallas_call(functools.partial(dense_kernel if dense_fits else slot_ker...]
where the time goes in v3:
time: 22.8 us; the launch traced here: 22.6 us
  Pallas kernels  20.4 us (89%)
  local copies, waits for them, and re-layouts  1.57 us (7%)
  between operations  0.66 us (3%)
    pallas_call x1, Pallas kernels, shards(): pl.pallas_call(functools.partial(dense_kernel if dense_fits else slot_ker...  20.4 us
    unnamed x1, local copies, waits for them, and re-layouts  1.57 us

profile of v3, /device:TPU:0, one launch (start us, length us, event | category | flops | bytes accessed | tf_op | source)
XLA Modules:
  0.0 22.6 jit_solution(17200666734711140976)
XLA Ops:
  0.7 20.4 %shard_map.73 = bf16[256,256]{1,0:T(8,128)(2,1)} custom-call(bf16[256,128]{1,0:T(8,128)(2,1)} %features.1, bf16[1,1,96,128,128]{4,3,2,1,0:T(8,128)(2,1)} %values.1, s32[1,1,96]{2,1,0:T(1,128)} %rows_in.1, s32[1,1,96]{2,1,0:T(1,128)} %cols_in.1, s32[1,1]{1,0:T(1,128)S(6)} %copy.9.counts, bf16[128,256]{1,0:T(8,128)(2,1)} %weight.1, f32[1,256]{1,0:T(1,128)} %bitcast.1), custom_call_target="tpu_custom_call" | custom-call | flops 402653184 | bytes 3145728 | tf_op jit(solution)/shard_map/pallas_call | solution.py:384
  21.0 1.6 %copy.10 = bf16[256,256]{1,0:T(8,128)(2,1)} copy(bf16[256,256]{1,0:T(8,128)(2,1)} %shard_map.73) | data formatting | bytes 262144

commit v4 on v3

--- a/solution.py
+++ b/solution.py
@@ -291,33 +291,27 @@
     lax.fori_loop(0, tile_rows, place, 0)
 
     own_copy.wait()
-    sources = [narrow] + [lax.rem(narrow + narrow_count - offset, narrow_count) for offset in range(1, narrow_count)]
-    turns = [0] + list(range(1, narrow_count - 1, 2)) + list(range(narrow_count - 1, 0, -2))
-    turns = list(dict.fromkeys(turns + list(range(narrow_count))))
-    for n, turn in enumerate(turns[:-1]):
-        if turn:
-            feature_copies[turn - 1].wait_recv()
-        source = sources[turn]
-
-        def multiply(d, carry):
-            here = pl.ds(pl.multiple_of(d * nodes, nodes), nodes)
-            product = jnp.dot(dense[source, here], panel[source], preferred_element_type=jnp.float32)
-            sums[here] = product if n == 0 else sums[here] + product
-            return carry
-
-        lax.fori_loop(0, wide_count, multiply, 0, unroll=True)
-    if turns[-1]:
-        feature_copies[turns[-1] - 1].wait_recv()
-    final = sources[turns[-1]]
+
+    def multiply(d, carry):
+        here = pl.ds(pl.multiple_of(d * nodes, nodes), nodes)
+        sums[here] = jnp.dot(dense[narrow, here], panel[narrow], preferred_element_type=jnp.float32)
+        return carry
+
+    lax.fori_loop(0, wide_count, multiply, 0, unroll=True)
+    for copy in feature_copies:
+        copy.wait_recv()
 
     def chunk_sum(d):
         here = pl.ds(pl.multiple_of(d * nodes, nodes), nodes)
-        product = jnp.dot(dense[final, here], panel[final], preferred_element_type=jnp.float32)
-        return product + sums[here] if narrow_count > 1 else product
-
-    pair_copies = []
-    for i, target in enumerate(targets):
-        pair_out[i] = chunk_sum(target * 2 + other)
+        total = sums[here]
+        for source in peers:
+            total = total + jnp.dot(dense[source, here], panel[source], preferred_element_type=jnp.float32)
+        return total
+
+    pair_copies, line_copies = [], []
+
+    def send_pair(i):
+        pair_out[i] = chunk_sum(targets[i] * 2 + other)
         copy = pltpu.make_async_remote_copy(
             src_ref=pair_out.at[i],
             dst_ref=pair_in.at[i],
@@ -329,26 +323,30 @@
         copy.start()
         pair_copies.append(copy)
 
-    line_copies = []
-    total = None
-    for i, target in enumerate(targets):
-        own = chunk_sum(target * 2 + core)
+    def send_line(i):
+        own = chunk_sum(targets[i] * 2 + core)
         pair_copies[i].wait_recv()
-        both = own + pair_in[i]
-        if i == groups - 1:
-            total = both
-        else:
-            line_out[i] = both.astype(jnp.bfloat16)
-            copy = pltpu.make_async_remote_copy(
-                src_ref=line_out.at[i],
-                dst_ref=line_in.at[i],
-                send_sem=line_send.at[i],
-                recv_sem=line_recv.at[i],
-                device_id={"wide": target * 2 + core},
-                device_id_type=MESH,
-            )
-            copy.start()
-            line_copies.append(copy)
+        line_out[i] = (own + pair_in[i]).astype(jnp.bfloat16)
+        copy = pltpu.make_async_remote_copy(
+            src_ref=line_out.at[i],
+            dst_ref=line_in.at[i],
+            send_sem=line_send.at[i],
+            recv_sem=line_recv.at[i],
+            device_id={"wide": targets[i] * 2 + core},
+            device_id_type=MESH,
+        )
+        copy.start()
+        line_copies.append(copy)
+
+    for i in range(min(2, groups)):
+        send_pair(i)
+    for i in range(groups - 1):
+        send_line(i)
+        if i + 2 < groups:
+            send_pair(i + 2)
+    total = chunk_sum(targets[-1] * 2 + core)
+    pair_copies[-1].wait_recv()
+    total = total + pair_in[groups - 1]
 
     for i, copy in enumerate(line_copies):
         copy.wait_recv()

time: 22.8 us -> 22.2 us (0.974)
  Pallas kernels: 20.4 us -> 19.8 us
    pallas_call x1, Pallas kernels: 20.4 us -> 19.8 us  [shards(): pl.pallas_call(functools.partial(dense_kernel if dense_fits else slot_ker...]
where the time goes in v4:
time: 22.2 us; the launch traced here: 22 us
  Pallas kernels  19.8 us (89%)
  local copies, waits for them, and re-layouts  1.57 us (7%)
  between operations  0.66 us (3%)
    pallas_call x1, Pallas kernels, shards(): pl.pallas_call(functools.partial(dense_kernel if dense_fits else slot_ker...  19.8 us
    unnamed x1, local copies, waits for them, and re-layouts  1.57 us

profile of v4, /device:TPU:0, one launch (start us, length us, event | category | flops | bytes accessed | tf_op | source)
XLA Modules:
  0.0 22.0 jit_solution(7310743813908014803)
XLA Ops:
  0.7 19.8 %shard_map.73 = bf16[256,256]{1,0:T(8,128)(2,1)} custom-call(bf16[256,128]{1,0:T(8,128)(2,1)} %features.1, bf16[1,1,96,128,128]{4,3,2,1,0:T(8,128)(2,1)} %values.1, s32[1,1,96]{2,1,0:T(1,128)} %rows_in.1, s32[1,1,96]{2,1,0:T(1,128)} %cols_in.1, s32[1,1]{1,0:T(1,128)S(6)} %copy.9.counts, bf16[128,256]{1,0:T(8,128)(2,1)} %weight.1, f32[1,256]{1,0:T(1,128)} %bitcast.1), custom_call_target="tpu_custom_call" | custom-call | flops 402653184 | bytes 3145728 | tf_op jit(solution)/shard_map/pallas_call | solution.py:382
  20.4 1.6 %copy.10 = bf16[256,256]{1,0:T(8,128)(2,1)} copy(bf16[256,256]{1,0:T(8,128)(2,1)} %shard_map.73) | data formatting | bytes 262144

commit v5 on v4

--- a/solution.py
+++ b/solution.py
@@ -308,7 +308,7 @@
             total = total + jnp.dot(dense[source, here], panel[source], preferred_element_type=jnp.float32)
         return total
 
-    pair_copies, line_copies = [], []
+    pair_copies, line_copies = {}, []
 
     def send_pair(i):
         pair_out[i] = chunk_sum(targets[i] * 2 + other)
@@ -321,40 +321,56 @@
             device_id_type=MESH,
         )
         copy.start()
-        pair_copies.append(copy)
-
-    def send_line(i):
+        pair_copies[i] = copy
+
+    def chip_sum(i):
         own = chunk_sum(targets[i] * 2 + core)
         pair_copies[i].wait_recv()
-        line_out[i] = (own + pair_in[i]).astype(jnp.bfloat16)
+        return own + pair_in[i]
+
+    def send_line(i, value, target):
+        line_out[i] = value.astype(jnp.bfloat16)
         copy = pltpu.make_async_remote_copy(
             src_ref=line_out.at[i],
             dst_ref=line_in.at[i],
             send_sem=line_send.at[i],
             recv_sem=line_recv.at[i],
-            device_id={"wide": targets[i] * 2 + core},
+            device_id={"wide": target * 2 + core},
             device_id_type=MESH,
         )
         copy.start()
         line_copies.append(copy)
 
-    for i in range(min(2, groups)):
-        send_pair(i)
-    for i in range(groups - 1):
-        send_line(i)
-        if i + 2 < groups:
-            send_pair(i + 2)
-    total = chunk_sum(targets[-1] * 2 + core)
-    pair_copies[-1].wait_recv()
-    total = total + pair_in[groups - 1]
-
-    for i, copy in enumerate(line_copies):
-        copy.wait_recv()
+    if groups == 4:
+        far, near = targets[0], targets[2]
+        send_pair(1)
+        send_pair(0)
+        send_line(0, chip_sum(1), near)
+        send_pair(2)
+        crossing = chip_sum(0)
+        send_line(1, chip_sum(2), near)
+        send_pair(3)
+        line_copies[0].wait_recv()
+        send_line(2, crossing + line_in[0].astype(jnp.float32), far)
+        total = chip_sum(3)
+        arriving = (1, 2)
+    else:
+        for i in range(min(2, groups)):
+            send_pair(i)
+        for i in range(groups - 1):
+            send_line(i, chip_sum(i), targets[i])
+            if i + 2 < groups:
+                send_pair(i + 2)
+        total = chip_sum(groups - 1)
+        arriving = range(groups - 1)
+
+    for i in arriving:
+        line_copies[i].wait_recv()
         total = total + line_in[i].astype(jnp.float32)
     mixed = jnp.dot(total.astype(jnp.bfloat16), weight[...], preferred_element_type=jnp.float32) + bias[...]
     out[...] = jnp.maximum(mixed, 0.0).astype(out.dtype)
 
-    for copy in feature_copies + pair_copies + line_copies:
+    for copy in feature_copies + list(pair_copies.values()) + line_copies:
         copy.wait_send()
 
 

time: 22.2 us -> 24 us (1.081)
  Pallas kernels: 19.8 us -> 21.6 us
    pallas_call x1, Pallas kernels: 19.8 us -> 21.6 us  [shards(): pl.pallas_call(functools.partial(dense_kernel if dense_fits else slot_ker...]
where the time goes in v5:
time: 24 us; the launch traced here: 23.8 us
  Pallas kernels  21.6 us (90%)
  local copies, waits for them, and re-layouts  1.57 us (7%)
  between operations  0.66 us (3%)
    pallas_call x1, Pallas kernels, shards(): pl.pallas_call(functools.partial(dense_kernel if dense_fits else slot_ker...  21.6 us
    unnamed x1, local copies, waits for them, and re-layouts  1.57 us

profile of v5, /device:TPU:0, one launch (start us, length us, event | category | flops | bytes accessed | tf_op | source)
XLA Modules:
  0.0 23.8 jit_solution(18396278079603213517)
XLA Ops:
  0.7 21.6 %shard_map.73 = bf16[256,256]{1,0:T(8,128)(2,1)} custom-call(bf16[256,128]{1,0:T(8,128)(2,1)} %features.1, bf16[1,1,96,128,128]{4,3,2,1,0:T(8,128)(2,1)} %values.1, s32[1,1,96]{2,1,0:T(1,128)} %rows_in.1, s32[1,1,96]{2,1,0:T(1,128)} %cols_in.1, s32[1,1]{1,0:T(1,128)S(6)} %copy.9.counts, bf16[128,256]{1,0:T(8,128)(2,1)} %weight.1, f32[1,256]{1,0:T(1,128)} %bitcast.1), custom_call_target="tpu_custom_call" | custom-call | flops 402653184 | bytes 3145728 | tf_op jit(solution)/shard_map/pallas_call | solution.py:398
  22.2 1.6 %copy.10 = bf16[256,256]{1,0:T(8,128)(2,1)} copy(bf16[256,256]{1,0:T(8,128)(2,1)} %shard_map.73) | data formatting | bytes 262144

commit v6 on v4

--- a/solution.py
+++ b/solution.py
@@ -311,7 +311,7 @@
     pair_copies, line_copies = [], []
 
     def send_pair(i):
-        pair_out[i] = chunk_sum(targets[i] * 2 + other)
+        pair_out[i] = chunk_sum(targets[i] * 2 + other).astype(pair_out.dtype)
         copy = pltpu.make_async_remote_copy(
             src_ref=pair_out.at[i],
             dst_ref=pair_in.at[i],
@@ -326,7 +326,7 @@
     def send_line(i):
         own = chunk_sum(targets[i] * 2 + core)
         pair_copies[i].wait_recv()
-        line_out[i] = (own + pair_in[i]).astype(jnp.bfloat16)
+        line_out[i] = (own + pair_in[i].astype(jnp.float32)).astype(jnp.bfloat16)
         copy = pltpu.make_async_remote_copy(
             src_ref=line_out.at[i],
             dst_ref=line_in.at[i],
@@ -346,7 +346,7 @@
             send_pair(i + 2)
     total = chunk_sum(targets[-1] * 2 + core)
     pair_copies[-1].wait_recv()
-    total = total + pair_in[groups - 1]
+    total = total + pair_in[groups - 1].astype(jnp.float32)
 
     for i, copy in enumerate(line_copies):
         copy.wait_recv()
@@ -402,8 +402,8 @@
             ),
             pltpu.VMEM((8, lanes), jnp.int32),
             pltpu.SMEM((8, lanes), jnp.int32),
-            pltpu.VMEM((groups, nodes, width), jnp.float32),
-            pltpu.VMEM((groups, nodes, width), jnp.float32),
+            pltpu.VMEM((groups, nodes, width), jnp.bfloat16 if dense_fits else jnp.float32),
+            pltpu.VMEM((groups, nodes, width), jnp.bfloat16 if dense_fits else jnp.float32),
             pltpu.VMEM((max(groups - 1, 1), nodes, width), jnp.bfloat16),
             pltpu.VMEM((max(groups - 1, 1), nodes, width), jnp.bfloat16),
             dma((chunks,)),

time: 22.2 us -> 22.1 us (level)
  no operation moved by 1% of the time
where the time goes in v6:
time: 22.1 us; the launch traced here: 21.9 us
  Pallas kernels  19.7 us (89%)
  local copies, waits for them, and re-layouts  1.57 us (7%)
  between operations  0.66 us (3%)
    pallas_call x1, Pallas kernels, shards(): pl.pallas_call(functools.partial(dense_kernel if dense_fits else slot_ker...  19.7 us
    unnamed x1, local copies, waits for them, and re-layouts  1.57 us

profile of v6, /device:TPU:0, one launch (start us, length us, event | category | flops | bytes accessed | tf_op | source)
XLA Modules:
  0.0 21.9 jit_solution(7550281437517147083)
XLA Ops:
  0.7 19.7 %shard_map.73 = bf16[256,256]{1,0:T(8,128)(2,1)} custom-call(bf16[256,128]{1,0:T(8,128)(2,1)} %features.1, bf16[1,1,96,128,128]{4,3,2,1,0:T(8,128)(2,1)} %values.1, s32[1,1,96]{2,1,0:T(1,128)} %rows_in.1, s32[1,1,96]{2,1,0:T(1,128)} %cols_in.1, s32[1,1]{1,0:T(1,128)S(6)} %copy.9.counts, bf16[128,256]{1,0:T(8,128)(2,1)} %weight.1, f32[1,256]{1,0:T(1,128)} %bitcast.1), custom_call_target="tpu_custom_call" | custom-call | flops 402653184 | bytes 3145728 | tf_op jit(solution)/shard_map/pallas_call | solution.py:382
  20.4 1.6 %copy.10 = bf16[256,256]{1,0:T(8,128)(2,1)} copy(bf16[256,256]{1,0:T(8,128)(2,1)} %shard_map.73) | data formatting | bytes 262144
